TPU v7x, 128 devices: a whole 4x4x4 slice. The times are simulated.
128 devices in a mesh: row: 8 (over z_hi, y), col: 8 (over z_lo, x), slab: 2 (over core).
Axes of the slice: x: 4, y: 4, z: 4 (z_hi: 2, z_lo: 2; z = z_hi * 2 + z_lo), core: 2. Of those that a mesh axis runs over, the one named last changes fastest.
Arguments:
- amplitudes: bfloat16 [56, 32, 56, 400], P('col', None, 'row', 'slab'), may hold values from -6 to 6
- integrals: bfloat16 [56, 400, 56, 400], P('row', 'slab', 'col'), may hold values from -0.0390625 to 0.0390625
Outputs:
- residual: float32 [56, 32, 56, 400], P('row', None, 'col', 'slab')
All inputs are finite; a program needn't handle non-finite values.
Results may differ from a plain program's by a relative error of at most 0.0003.
Values may be sent and summed in bfloat16 or wider, within the bound.
No kernel may reach another device: no remote copies, remote signals or barrier semaphores. Data moves between devices by JAX's collectives and lax.ppermute only.
A program may use at most 192 MiB of HBM per device.

v0:
```python
import jax
import jax.numpy as jnp
from jax import lax
from jax.sharding import PartitionSpec as P


def partner(value, axis, stride):
    mask = 2**stride
    pairs = [(source, source ^ mask) for source in range(lax.axis_size(axis))]
    return lax.ppermute(value, axis, pairs)


def on_device(amplitudes, integrals):
    gathered = lax.all_gather(amplitudes, "col", axis=0, tiled=True)
    occupied, slab_width, inner_occ, inner_virt = gathered.shape
    inner_size = inner_occ * inner_virt
    out_occ = integrals.shape[2]
    out_virt = integrals.shape[3]
    weight_matrix = integrals.reshape(inner_size, out_occ * out_virt)
    amp_matrix = gathered.reshape(occupied * slab_width, inner_size)
    own_rows = occupied // lax.axis_size("row")
    product = jnp.dot(amp_matrix, weight_matrix, preferred_element_type=jnp.float32)
    summed = lax.psum_scatter(
        lax.psum_scatter(
            product.reshape(own_rows * lax.axis_size("row"), slab_width, out_occ, out_virt),
            "row",
            scatter_dimension=0,
            tiled=True,
        ),
        "slab",
        scatter_dimension=3,
        tiled=True,
    )
    row_index = lax.axis_index("row")
    col_index = lax.axis_index("col")
    bit_count = lax.axis_size("col").bit_length() - 1
    mirrored = summed
    for bit_number in range(bit_count):
        moved_block = mirrored
        for offset in (0, bit_count):
            moved_block = partner(moved_block, ("row", "col"), bit_number + offset)
        differs = row_index >> bit_number & 1 != col_index >> bit_number & 1
        mirrored = jnp.where(differs, moved_block, mirrored)
    return summed - jnp.transpose(mirrored, (2, 1, 0, 3))


def solution(mesh):
    return jax.shard_map(
        on_device,
        mesh=mesh,
        in_specs=(P("col", None, "row", "slab"), P("row", "slab", "col", None)),
        out_specs=P("row", None, "col", "slab"),
        check_vma=False,
    )
```

profile of v0, /device:TPU:14, one launch (start us, length us, event | category | flops | bytes accessed | tf_op | source)
XLA Modules:
  0.0 670.4 jit_solution(1137520847818517)
XLA Ops:
  7.3 16.7 %copy.17 = bf16[7,200,7,400]{3,2,1,0:T(8,128)(2,1)} copy(bf16[7,200,7,400]{3,1,2,0:T(8,128)(2,1)} %param.3) | data formatting | bytes 15680000 | tf_op args[1]
  24.0 19.1 %reshape.8 = bf16[1400,2800]{1,0:T(8,128)(2,1)} reshape(bf16[7,200,7,400]{3,2,1,0:T(8,128)(2,1)} %copy.17) | data formatting | bytes 15680000 | tf_op jit(solution)/shard_map/reshape | solution.py:19
  43.1 11.4 %copy.18 = bf16[2800,1400]{1,0:T(8,128)(2,1)} copy(bf16[2800,1400]{0,1:T(8,128)(2,1)} %bitcast.15) | data formatting | bytes 15680000 | tf_op jit(solution)/shard_map/dot_general | solution.py:22
  54.5 28.1 %all-gather.2.cloned.1.call-done = bf16[56,32,7,200]{3,1,2,0:T(8,128)(2,1)} async-done(((bf16[7,32,7,200]{3,1,2,0:T(8,128)(2,1)}), bf16[56,32,7,200]{3,1,2,0:T(8,128)(2,1)}) %all-gather.2.cloned.1.call-update) | async-done | bytes 5017616 | tf_op jit(solution)/shard_map/all_gather | solution.py:14
  82.6 13.4 %copy.16 = bf16[56,32,7,200]{3,2,1,0:T(8,128)(2,1)} copy(bf16[56,32,7,200]{3,1,2,0:T(8,128)(2,1)} %all-gather.2.cloned.1.call-done) | data formatting | bytes 10035200 | tf_op jit(solution)/shard_map/all_gather | solution.py:14
  96.0 12.1 %reshape.9 = bf16[56,32,1400,1]{2,1,0,3:T(8,128)(2,1)} reshape(bf16[56,32,7,200]{3,2,1,0:T(8,128)(2,1)} %copy.16) | data formatting | bytes 10035200 | tf_op jit(solution)/shard_map/dot_general | solution.py:22
  108.1 26.8 %fusion = f32[56,32,7,400]{3,1,2,0:T(8,128)} fusion(bf16[7,400,1400,1]{2,1,0,3:T(8,128)(2,1)} %bitcast.16, bf16[56,32,1400,1]{2,1,0,3:T(8,128)(2,1)} %reshape.9), kind=kOutput, calls=%fused_computation | convolution fusion | flops 14049280000 | bytes 32928000 | tf_op jit(solution)/shard_map/dot_general | solution.py:22
  135.0 267.9 %reduce-scatter.3.cloned.1.call-done = f32[7,32,7,400]{3,1,2,0:T(8,128)} async-done(((f32[56,32,7,400]{3,1,2,0:T(8,128)}), f32[7,32,7,400]{3,1,2,0:T(8,128)}) %reduce-scatter.3.cloned.1.call-update) | async-done | bytes 2508816 | tf_op jit(solution)/shard_map/reduce_scatter | solution.py:24
  404.8 30.2 %all-reduce.3.cloned.1.call-done = f32[7,32,7,400]{3,1,2,0:T(8,128)} async-done(((f32[7,32,7,400]{3,1,2,0:T(8,128)}), f32[7,32,7,400]{3,1,2,0:T(8,128)}) %all-reduce.3.cloned.1.call-update) | async-done | bytes 2508816
  435.1 2.2 constant_dynamic-slice_fusion
  438.3 36.5 %collective-permute-done = f32[7,32,7,200]{3,1,0,2:T(8,128)} collective-permute-done((f32[7,32,7,200]{3,1,0,2:T(8,128)S(1)}, f32[7,32,7,200]{3,1,0,2:T(8,128)}, u32[]{:S(2)}, u32[]{:S(2)}) %collective-permute-start) | collective-permute-done | bytes 1254432 | tf_op jit(solution)/shard_map/ppermute | solution.py:10
  475.4 36.3 %collective-permute-done.1 = f32[7,32,7,200]{3,1,0,2:T(8,128)} collective-permute-done((f32[7,32,7,200]{3,1,0,2:T(8,128)}, f32[7,32,7,200]{3,1,0,2:T(8,128)}, u32[]{:S(2)}, u32[]{:S(2)}) %collective-permute-start.1) | collective-permute-done | bytes 1254432 | tf_op jit(solution)/shard_map/ppermute | solution.py:10
  512.2 1.1 copy-done.2
  513.3 1.5 collective-permute-start.2
  514.8 35.8 %collective-permute-done.2 = f32[7,32,7,200]{3,1,0,2:T(8,128)} collective-permute-done((f32[7,32,7,200]{3,1,0,2:T(8,128)S(1)}, f32[7,32,7,200]{3,1,0,2:T(8,128)}, u32[]{:S(2)}, u32[]{:S(2)}) %collective-permute-start.2) | collective-permute-done | bytes 1254432 | tf_op jit(solution)/shard_map/ppermute | solution.py:10
  550.6 2.1 collective-permute-start.3
  552.7 34.4 %collective-permute-done.3 = f32[7,32,7,200]{3,1,0,2:T(8,128)} collective-permute-done((f32[7,32,7,200]{3,1,0,2:T(8,128)}, f32[7,32,7,200]{3,1,0,2:T(8,128)}, u32[]{:S(2)}, u32[]{:S(2)}) %collective-permute-start.3) | collective-permute-done | bytes 1254432 | tf_op jit(solution)/shard_map/ppermute | solution.py:10
  587.1 1.7 broadcast_select_fusion.1
  588.8 1.1 copy-done.1
  590.0 1.6 collective-permute-start.4
  591.5 32.3 %collective-permute-done.4 = f32[7,32,7,200]{3,1,0,2:T(8,128)} collective-permute-done((f32[7,32,7,200]{3,1,0,2:T(8,128)S(1)}, f32[7,32,7,200]{3,1,0,2:T(8,128)}, u32[]{:S(2)}, u32[]{:S(2)}) %collective-permute-start.4) | collective-permute-done | bytes 1254432 | tf_op jit(solution)/shard_map/ppermute | solution.py:10
  623.9 3.9 collective-permute-start.5
  627.7 32.9 %collective-permute-done.5 = f32[7,32,7,200]{3,1,0,2:T(8,128)} collective-permute-done((f32[7,32,7,200]{3,1,0,2:T(8,128)}, f32[7,32,7,200]{3,1,0,2:T(8,128)}, u32[]{:S(2)}, u32[]{:S(2)}) %collective-permute-start.5) | collective-permute-done | bytes 1254432 | tf_op jit(solution)/shard_map/ppermute | solution.py:10
  660.6 3.2 bitcast_subtract_fusion
  (17 shorter events, 4.2 us)
Async XLA Ops:
  6.5 76.1 %all-gather.2.cloned.1.call-start = ((), (), s32[]{:S(2)}) async-start(), calls=%async_computation.1 | async-start | bytes 7225344 | tf_op jit(solution)/shard_map/all_gather | solution.py:14
  7.3 395.7 %reduce-scatter.3.cloned.1.call-start = ((), (), s32[]{:S(2)}) async-start(), calls=%async_computation.2 | async-start | bytes 28901376 | tf_op jit(solution)/shard_map/reduce_scatter | solution.py:24
  135.0 300.1 %all-reduce.3.cloned.1.call-start = ((), (), s32[]{:S(2)}) async-start(), calls=%async_computation.3 | async-start | bytes 6422528
  402.9 0.7 copy-start.3
  437.2 74.5 %copy-start = (f32[7,32,7,400]{3,1,2,0:T(8,128)S(1)}, f32[7,32,7,400]{3,1,2,0:T(8,128)}, u32[]{:S(2)}) copy-start(f32[7,32,7,400]{3,1,2,0:T(8,128)} %all-reduce.3.cloned.1.call-done) | copy-start | bytes 7526404
  437.4 37.5 %collective-permute-start = (f32[7,32,7,200]{3,1,0,2:T(8,128)S(1)}, f32[7,32,7,200]{3,1,0,2:T(8,128)}, u32[]{:S(2)}, u32[]{:S(2)}) collective-permute-start(f32[7,32,7,200]{3,1,0,2:T(8,128)S(1)} %copy.19), channel_id=1, source_target_pairs={{0,2},{2,0},{4,6},{6,4},{8,10},{10,8},{12,14},{14,12},{16,18},{18,... | collective-permute-start | bytes 3763208 | tf_op jit(solution)/shard_map/ppermute | solution.py:10
  474.9 36.8 %collective-permute-start.1 = (f32[7,32,7,200]{3,1,0,2:T(8,128)}, f32[7,32,7,200]{3,1,0,2:T(8,128)}, u32[]{:S(2)}, u32[]{:S(2)}) collective-permute-start(f32[7,32,7,200]{3,1,0,2:T(8,128)} %collective-permute-done), channel_id=1, source_target_pairs={{0,16},{2,18},{4,20},{6,22},{8,24},{10,26},{12,28},{14,30},{16,0},... | collective-permute-start | bytes 3763208 | tf_op jit(solution)/shard_map/ppermute | solution.py:10
  512.2 1.2 copy-start.2
  513.3 37.2 %collective-permute-start.2 = (f32[7,32,7,200]{3,1,0,2:T(8,128)S(1)}, f32[7,32,7,200]{3,1,0,2:T(8,128)}, u32[]{:S(2)}, u32[]{:S(2)}) collective-permute-start(f32[7,32,7,200]{3,1,0,2:T(8,128)S(1)} %broadcast_select_fusion), channel_id=1, source_target_pairs={{0,4},{2,6},{4,0},{6,2},{8,12},{10,14},{12,8},{14,10},{16,20},{18,... | collective-permute-start | bytes 3763208 | tf_op jit(solution)/shard_map/ppermute | solution.py:10
  550.6 36.5 %collective-permute-start.3 = (f32[7,32,7,200]{3,1,0,2:T(8,128)}, f32[7,32,7,200]{3,1,0,2:T(8,128)}, u32[]{:S(2)}, u32[]{:S(2)}) collective-permute-start(f32[7,32,7,200]{3,1,0,2:T(8,128)} %collective-permute-done.2), channel_id=1, source_target_pairs={{0,32},{2,34},{4,36},{6,38},{8,40},{10,42},{12,44},{14,46},{16,48}... | collective-permute-start | bytes 3763208 | tf_op jit(solution)/shard_map/ppermute | solution.py:10
  588.8 1.2 copy-start.1
  590.0 33.9 %collective-permute-start.4 = (f32[7,32,7,200]{3,1,0,2:T(8,128)S(1)}, f32[7,32,7,200]{3,1,0,2:T(8,128)}, u32[]{:S(2)}, u32[]{:S(2)}) collective-permute-start(f32[7,32,7,200]{3,1,0,2:T(8,128)S(1)} %broadcast_select_fusion.1), channel_id=1, source_target_pairs={{0,8},{2,10},{4,12},{6,14},{8,0},{10,2},{12,4},{14,6},{16,24},{18,... | collective-permute-start | bytes 3763208 | tf_op jit(solution)/shard_map/ppermute | solution.py:10
  623.9 36.8 %collective-permute-start.5 = (f32[7,32,7,200]{3,1,0,2:T(8,128)}, f32[7,32,7,200]{3,1,0,2:T(8,128)}, u32[]{:S(2)}, u32[]{:S(2)}) collective-permute-start(f32[7,32,7,200]{3,1,0,2:T(8,128)} %collective-permute-done.4), channel_id=1, source_target_pairs={{0,64},{2,66},{4,68},{6,70},{8,72},{10,74},{12,76},{14,78},{16,80}... | collective-permute-start | bytes 3763208 | tf_op jit(solution)/shard_map/ppermute | solution.py:10
Sparse Core Ops, SparseCore 0:
  9.0 73.5 all-gather.1
  135.1 267.8 reduce-scatter.2
  405.6 29.4 all-reduce.2
where the time goes:
time: 673 us; the launch traced here: 670 us
  waiting for transfers between devices  535 us (79%)
  local copies, waits for them, and re-layouts  78.5 us (12%)
  matrix products  26.8 us (4%)
  between operations  13.8 us (2%)
  starting transfers between devices  10.6 us (2%)
    reduce_scatter x1, waiting for transfers between devices, on_device(): lax.psum_scatter(product.reshape(own_rows * lax.axis_size('row'), slab_wi...  268 us
    ppermute x6, waiting for transfers between devices, partner(): return lax.ppermute(value, axis, pairs)  208 us
    unnamed x4, waiting for transfers between devices  31 us
    all_gather x1, waiting for transfers between devices, on_device(): gathered = lax.all_gather(amplitudes, 'col', axis=0, tiled=True)  28.1 us
    dot_general x1, matrix products, on_device(): jnp.dot(amp_matrix, weight_matrix, preferred_element_type=jnp.float32)  26.8 us
    dot_general x2, local copies, waits for them, and re-layouts, on_device(): jnp.dot(amp_matrix, weight_matrix, preferred_element_type=jnp.float32)  23.5 us
    unnamed x11, local copies, waits for them, and re-layouts  22.4 us
    reshape x1, local copies, waits for them, and re-layouts, on_device(): weight_matrix = integrals.reshape(inner_size, out_occ * out_virt)  19.1 us
  transfers between devices with their start and end apart: 9, of which 9 were waited for; matrix products, arithmetic and copies ran while one was open for 7% of the time, Pallas kernels for 0%

commit v1 on v0

v1 whole, which is shorter than its diff:
```python
import jax
import jax.numpy as jnp
from jax import lax
from jax.experimental import pallas as pl
from jax.experimental.pallas import tpu as pltpu
from jax.sharding import PartitionSpec as P

CHUNKS = (1, 2, 2, 2)
LANE = 128
GAIN = 2.0**7.875
VMEM = 60 * 1024 * 1024


def padded(size):
    return -(-size // LANE) * LANE


def whole():
    return pl.BlockSpec(memory_space=pltpu.VMEM)


def params():
    return pltpu.CompilerParams(vmem_limit_bytes=VMEM)


def encode(values, used):
    top = jnp.max(jnp.abs(values), axis=1, keepdims=True)
    scale = jnp.maximum(top, 1e-30).astype(jnp.bfloat16).astype(jnp.float32)
    t = values * (GAIN / scale)
    t2 = t * t
    t4 = t2 * t2
    t8 = t4 * t4
    power = t8 * t8
    power = jnp.where(values < 0, -power, power)
    lanes = lax.broadcasted_iota(jnp.int32, values.shape, 1)
    return jnp.where(lanes == used, scale, power).astype(jnp.bfloat16)


def decode(coded, used):
    y = coded.astype(jnp.float32)
    scale = y[:, used : used + 1] * (1.0 / GAIN)
    root = lax.rsqrt(lax.rsqrt(lax.rsqrt(lax.rsqrt(jnp.abs(y)))))
    value = jnp.where(y < 0, -root, root) * scale
    lanes = lax.broadcasted_iota(jnp.int32, y.shape, 1)
    return jnp.where(lanes < used, value, 0.0)


def pack_amplitudes(x):
    occ, inner, width, virt = x.shape
    lanes = padded(inner * virt)

    def kernel(x_ref, *out_refs):
        first = 0
        for out_ref, count in zip(out_refs, CHUNKS):
            for i in range(count):
                rows = slice(i * width, (i + 1) * width)
                out_ref[rows, lanes - LANE :] = jnp.zeros((width, LANE), out_ref.dtype)
                for k in range(inner):
                    out_ref[rows, k * virt : (k + 1) * virt] = x_ref[first + i, k]
            first += count

    return pl.pallas_call(
        kernel,
        out_shape=[jax.ShapeDtypeStruct((count * width, lanes), x.dtype) for count in CHUNKS],
        in_specs=[whole()],
        out_specs=[whole() for _ in CHUNKS],
        compiler_params=params(),
    )(x)


def pack_integrals(slab, w):
    inner, outer, virt, wide = w.shape
    half = wide // 2
    rows = padded(inner * virt)
    lanes = padded(outer * half)

    def kernel(slab_ref, w_ref, mine_ref, other_ref):
        step = pl.program_id(0)
        low = slab_ref[0] == 0

        @pl.when(step == 0)
        def _():
            for out_ref in (mine_ref, other_ref):
                out_ref[:, lanes - LANE :] = jnp.zeros((rows, LANE), out_ref.dtype)
                out_ref[rows - 16 :, :] = jnp.zeros((16, lanes), out_ref.dtype)

        for k in range(inner):

            @pl.when(step == k)
            def _():
                for j in range(outer):
                    first, second = w_ref[0, j, :, :half], w_ref[0, j, :, half:]
                    at = (slice(k * virt, (k + 1) * virt), slice(j * half, (j + 1) * half))
                    mine_ref[at] = jnp.where(low, first, second)
                    other_ref[at] = jnp.where(low, second, first)

    shape = jax.ShapeDtypeStruct((rows, lanes), w.dtype)
    spec = pl.BlockSpec((rows, lanes), lambda k, s: (0, 0))
    return pl.pallas_call(
        kernel,
        out_shape=[shape, shape],
        grid_spec=pltpu.PrefetchScalarGridSpec(
            num_scalar_prefetch=1,
            grid=(inner,),
            in_specs=[pl.BlockSpec((1, outer, virt, wide), lambda k, s: (k, 0, 0, 0))],
            out_specs=[spec, spec],
        ),
        compiler_params=params(),
    )(slab, w)


def multiply(slab, gathered, mine, other, used):
    blocks, slabs, rows, _ = gathered.shape
    depth, lanes = mine.shape
    per_step = max(1, 256 // rows)

    def kernel(slab_ref, g_ref, mine_ref, other_ref, out_ref):
        own = slab_ref[0]

        def part(which):
            return g_ref[:, pl.ds(which, 1), :, :].reshape(per_step * rows, depth)

        total = jnp.dot(part(own), mine_ref[...], preferred_element_type=jnp.float32)
        total += jnp.dot(part(1 - own), other_ref[...], preferred_element_type=jnp.float32)
        out_ref[...] = encode(total, used).reshape(per_step, rows, lanes)

    return pl.pallas_call(
        kernel,
        out_shape=jax.ShapeDtypeStruct((blocks, rows, lanes), jnp.bfloat16),
        grid_spec=pltpu.PrefetchScalarGridSpec(
            num_scalar_prefetch=1,
            grid=(blocks // per_step,),
            in_specs=[
                pl.BlockSpec((per_step, slabs, rows, gathered.shape[3]), lambda n, s: (n, 0, 0, 0)),
                pl.BlockSpec((depth, lanes), lambda n, s: (0, 0)),
                pl.BlockSpec((depth, lanes), lambda n, s: (0, 0)),
            ],
            out_specs=pl.BlockSpec((per_step, rows, lanes), lambda n, s: (n, 0, 0)),
        ),
        compiler_params=params(),
    )(slab, gathered, mine, other)


def add_up(received, used):
    blocks, rows, lanes = received.shape

    def kernel(x_ref, sum_ref, coded_ref):
        total = decode(x_ref[0], used)
        for n in range(1, blocks):
            total += decode(x_ref[n], used)
        sum_ref[...] = total
        coded_ref[...] = encode(total, used)

    return pl.pallas_call(
        kernel,
        out_shape=[
            jax.ShapeDtypeStruct((rows, lanes), jnp.float32),
            jax.ShapeDtypeStruct((rows, lanes), jnp.bfloat16),
        ],
        in_specs=[whole()],
        out_specs=[whole(), whole()],
        compiler_params=params(),
    )(received)


def subtract(sums, mirrored, width, occ, virt):
    used = occ * virt
    count = len(sums)

    def kernel(*refs):
        sum_refs, mirror_refs, out_ref, flat = refs[:count], refs[count : 2 * count], refs[-2], refs[-1]
        first = 0
        for ref, n in zip(mirror_refs, CHUNKS):
            flat[first * width : (first + n) * width, :] = decode(ref[...], used)
            first += n
        first = 0
        for ref, n in zip(sum_refs, CHUNKS):
            for i in range(n):
                for j in range(occ):
                    own = ref[i * width : (i + 1) * width, j * virt : (j + 1) * virt]
                    at = first + i
                    out_ref[at, j] = own - flat[j * width : (j + 1) * width, at * virt : (at + 1) * virt]
            first += n

    return pl.pallas_call(
        kernel,
        out_shape=jax.ShapeDtypeStruct((occ, occ, width, virt), jnp.float32),
        in_specs=[whole() for _ in range(2 * count)],
        out_specs=whole(),
        scratch_shapes=[pltpu.VMEM((occ * width, sums[0].shape[1]), jnp.float32)],
        compiler_params=params(),
    )(*sums, *mirrored)


def on_device(amplitudes, integrals):
    occ, width, _, _ = amplitudes.shape
    out_occ = integrals.shape[2]
    out_virt = integrals.shape[3] // lax.axis_size("slab")
    used = out_occ * out_virt
    rows, cols = lax.axis_size("row"), lax.axis_size("col")
    slab = lax.axis_index("slab").astype(jnp.int32).reshape(1)
    mirror_pairs = [(r * cols + c, c * cols + r) for r in range(rows) for c in range(cols)]

    packed = pack_amplitudes(jnp.transpose(amplitudes, (0, 2, 1, 3)))
    gathered = []
    for chunk in packed:
        if gathered:
            chunk, _ = lax.optimization_barrier((chunk, gathered[-1]))
        gathered.append(lax.all_gather(chunk, ("col", "slab"), axis=0))
    mine, sent = pack_integrals(slab, jnp.transpose(integrals, (0, 2, 1, 3)))
    other = lax.ppermute(sent, "slab", [(0, 1), (1, 0)])

    sums, mirrored = [], []
    for chunk in gathered:
        chunk = chunk.reshape(cols, 2, chunk.shape[1], chunk.shape[2])
        coded = multiply(slab, chunk, mine, other, used)
        received = lax.all_to_all(coded, "row", 0, 0, tiled=True)
        total, again = add_up(received, used)
        sums.append(total)
        mirrored.append(lax.ppermute(again, ("row", "col"), mirror_pairs))
    residual = subtract(sums, mirrored, width, occ, out_virt)
    return jnp.transpose(residual, (0, 2, 1, 3))


def solution(mesh):
    return jax.shard_map(
        on_device,
        mesh=mesh,
        in_specs=(P("col", None, "row", "slab"), P("row", "slab", "col", None)),
        out_specs=P("row", None, "col", "slab"),
        check_vma=False,
    )
```

time: 673 us -> 273 us (0.41)
  waiting for transfers between devices: 535 us -> 130 us
  Pallas kernels: 0 us -> 77.5 us
  local copies, waits for them, and re-layouts: 78.5 us -> 1.7 us
  starting transfers between devices: 10.6 us -> 50.2 us
  matrix products: 26.8 us -> 0 us
    reduce_scatter x1 -> x0, waiting for transfers between devices: 268 us -> none  [on_device(): lax.psum_scatter(product.reshape(own_rows * lax.axis_size('row'), slab_wi...]
    ppermute x6 -> x5, waiting for transfers between devices: 208 us -> 14.4 us  [the longest x1 7.3 us: on_device(): other = lax.ppermute(sent, 'slab', [(0, 1), (1, 0)])]
    pallas_call x0 -> x11, Pallas kernels: none -> 77.5 us  [the longest x4 40.3 us: multiply(): pl.pallas_call(kernel, out_shape=jax.ShapeDtypeStruct((blocks, rows, lane...]
    all_gather x1 -> x4, waiting for transfers between devices: 28.1 us -> 102 us  [on_device(): gathered.append(lax.all_gather(chunk, ('col', 'slab'), axis=0))]
    all_to_all x0 -> x4, starting transfers between devices: none -> 31.6 us  [on_device(): received = lax.all_to_all(coded, 'row', 0, 0, tiled=True)]
    unnamed x4, waiting for transfers between devices: 31 us -> 1.95 us
    dot_general x1 -> x0, matrix products: 26.8 us -> none  [on_device(): jnp.dot(amp_matrix, weight_matrix, preferred_element_type=jnp.float32)]
    dot_general x2 -> x0, local copies, waits for them, and re-layouts: 23.5 us -> none  [on_device(): jnp.dot(amp_matrix, weight_matrix, preferred_element_type=jnp.float32)]
  transfers between devices with their start and end apart: 9 -> 13, of which waited for: 9 -> 7; matrix products, arithmetic and copies ran while one was open for 7% -> 0% of each run, Pallas kernels for 0% -> 26%
where the time goes in v1:
time: 273 us; the launch traced here: 272 us
  waiting for transfers between devices  130 us (48%)
  Pallas kernels  77.5 us (28%)
  starting transfers between devices  50.2 us (18%)
  between operations  13.2 us (5%)
    all_gather x4, waiting for transfers between devices, on_device(): gathered.append(lax.all_gather(chunk, ('col', 'slab'), axis=0))  102 us
    pallas_call x4, Pallas kernels, multiply(): pl.pallas_call(kernel, out_shape=jax.ShapeDtypeStruct((blocks, rows, lane...  40.3 us
    all_to_all x4, starting transfers between devices, on_device(): received = lax.all_to_all(coded, 'row', 0, 0, tiled=True)  31.6 us
    ppermute x4, starting transfers between devices, on_device(): mirrored.append(lax.ppermute(again, ('row', 'col'), mirror_pairs))  18.6 us
    pallas_call x1, Pallas kernels, pack_integrals(): pl.pallas_call(kernel, out_shape=[shape, shape], grid_spec=pltpu.Prefetch...  16.1 us
    pallas_call x4, Pallas kernels, add_up(): pl.pallas_call(kernel, out_shape=[jax.ShapeDtypeStruct((rows, lanes), jnp...  13.7 us
    all_to_all x4, waiting for transfers between devices, on_device(): received = lax.all_to_all(coded, 'row', 0, 0, tiled=True)  10.8 us
    ppermute x1, waiting for transfers between devices, on_device(): other = lax.ppermute(sent, 'slab', [(0, 1), (1, 0)])  7.3 us
  transfers between devices with their start and end apart: 13, of which 7 were waited for; matrix products, arithmetic and copies ran while one was open for 0% of the time, Pallas kernels for 26%

profile of v1, /device:TPU:14, one launch (start us, length us, event | category | flops | bytes accessed | tf_op | source)
XLA Modules:
  0.0 272.2 jit_solution(8384206571942891079)
XLA Ops:
  10.1 16.1 %shard_map.29 = (bf16[1408,1408]{1,0:T(8,128)(2,1)}, bf16[1408,1408]{1,0:T(8,128)(2,1)}) custom-call(s32[1]{0:T(128)} %bitcast.slab_ref, bf16[7,7,200,400]{3,2,1,0:T(8,128)(2,1)} %bitcast.8), custom_call_target="tpu_custom_call" | custom-call | tf_op jit(solution)/shard_map/pallas_call | solution.py:99
  26.3 7.3 %collective-permute-done.other_ref = bf16[1408,1408]{1,0:T(8,128)(2,1)} collective-permute-done((bf16[1408,1408]{1,0:T(8,128)(2,1)}, bf16[1408,1408]{1,0:T(8,128)(2,1)}, u32[]{:S(2)}, u32[]{:S(2)}) %collective-permute-start) | collective-permute-done | bytes 3964960 | tf_op jit(solution)/shard_map/ppermute | solution.py:211
  33.6 12.3 %all-gather.15.cloned.1.call-done = bf16[1024,1408]{1,0:T(8,128)(2,1)} async-done(((bf16[64,1408]{1,0:T(8,128)(2,1)}), bf16[1024,1408]{1,0:T(8,128)(2,1)}) %all-gather.15.cloned.1.call-update) | async-done | bytes 2883600 | tf_op jit(solution)/shard_map/all_gather | solution.py:209
  45.9 10.8 %shard_map.36 = bf16[8,64,1408]{2,1,0:T(8,128)(2,1)} custom-call(s32[1]{0:T(128)} %bitcast.slab_ref, bf16[8,2,64,1408]{3,2,1,0:T(8,128)(2,1)} %bitcast.11, bf16[1408,1408]{1,0:T(8,128)(2,1)} %get-tuple-element.23.mine_ref, bf16[1408,1408]{1,0:T(8,128)(2,1)} %collective-permute-done.other_ref), custom_call_target="tpu_custom_call" | custom-call | tf_op jit(solution)/shard_map/pallas_call | solution.py:127
  56.7 7.2 %all-to-all-start.3 = ((bf16[8,64,1408]{2,1,0:T(8,128)(2,1)}), bf16[8,64,1408]{2,1,0:T(8,128)(2,1)S(1)}, u32[]{:S(2)}, u32[]{:S(2)}) async-start(bf16[8,64,1408]{2,1,0:T(8,128)(2,1)} %shard_map.36), calls=%async_computation.3 | async-start | bytes 2883584 | tf_op jit(solution)/shard_map/all_to_all | solution.py:217
  64.5 31.5 %all-gather.13.cloned.1.call-done = bf16[1024,1408]{1,0:T(8,128)(2,1)} async-done(((bf16[64,1408]{1,0:T(8,128)(2,1)}), bf16[1024,1408]{1,0:T(8,128)(2,1)}) %all-gather.13.cloned.1.call-update) | async-done | bytes 2883600 | tf_op jit(solution)/shard_map/all_gather | solution.py:209
  96.0 10.8 %shard_map.34 = bf16[8,64,1408]{2,1,0:T(8,128)(2,1)} custom-call(s32[1]{0:T(128)} %bitcast.slab_ref, bf16[8,2,64,1408]{3,2,1,0:T(8,128)(2,1)} %bitcast.10, bf16[1408,1408]{1,0:T(8,128)(2,1)} %get-tuple-element.23.mine_ref, bf16[1408,1408]{1,0:T(8,128)(2,1)} %collective-permute-done.other_ref), custom_call_target="tpu_custom_call" | custom-call | tf_op jit(solution)/shard_map/pallas_call | solution.py:127
  106.8 7.6 %all-to-all-start.2 = ((bf16[8,64,1408]{2,1,0:T(8,128)(2,1)}), bf16[8,64,1408]{2,1,0:T(8,128)(2,1)S(1)}, u32[]{:S(2)}, u32[]{:S(2)}) async-start(bf16[8,64,1408]{2,1,0:T(8,128)(2,1)} %shard_map.34), calls=%async_computation.2 | async-start | bytes 2883584 | tf_op jit(solution)/shard_map/all_to_all | solution.py:217
  114.4 32.1 %all-gather.11.cloned.1.call-done = bf16[1024,1408]{1,0:T(8,128)(2,1)} async-done(((bf16[64,1408]{1,0:T(8,128)(2,1)}), bf16[1024,1408]{1,0:T(8,128)(2,1)}) %all-gather.11.cloned.1.call-update) | async-done | bytes 2883600 | tf_op jit(solution)/shard_map/all_gather | solution.py:209
  146.5 10.8 %shard_map.32 = bf16[8,64,1408]{2,1,0:T(8,128)(2,1)} custom-call(s32[1]{0:T(128)} %bitcast.slab_ref, bf16[8,2,64,1408]{3,2,1,0:T(8,128)(2,1)} %bitcast.9, bf16[1408,1408]{1,0:T(8,128)(2,1)} %get-tuple-element.23.mine_ref, bf16[1408,1408]{1,0:T(8,128)(2,1)} %collective-permute-done.other_ref), custom_call_target="tpu_custom_call" | custom-call | tf_op jit(solution)/shard_map/pallas_call | solution.py:127
  157.3 7.6 %all-to-all-start.1 = ((bf16[8,64,1408]{2,1,0:T(8,128)(2,1)}), bf16[8,64,1408]{2,1,0:T(8,128)(2,1)S(1)}, u32[]{:S(2)}, u32[]{:S(2)}) async-start(bf16[8,64,1408]{2,1,0:T(8,128)(2,1)} %shard_map.32), calls=%async_computation.1 | async-start | bytes 2883584 | tf_op jit(solution)/shard_map/all_to_all | solution.py:217
  164.9 26.5 %all-gather.9.cloned.1.call-done = bf16[512,1408]{1,0:T(8,128)(2,1)} async-done(((bf16[32,1408]{1,0:T(8,128)(2,1)}), bf16[512,1408]{1,0:T(8,128)(2,1)}) %all-gather.9.cloned.1.call-update) | async-done | bytes 1441808 | tf_op jit(solution)/shard_map/all_gather | solution.py:209
  191.4 7.8 %shard_map.30 = bf16[8,32,1408]{2,1,0:T(8,128)(2,1)} custom-call(s32[1]{0:T(128)} %bitcast.slab_ref, bf16[8,2,32,1408]{3,2,1,0:T(8,128)(2,1)} %bitcast.12, bf16[1408,1408]{1,0:T(8,128)(2,1)} %get-tuple-element.23.mine_ref, bf16[1408,1408]{1,0:T(8,128)(2,1)} %collective-permute-done.other_ref), custom_call_target="tpu_custom_call" | custom-call | tf_op jit(solution)/shard_map/pallas_call | solution.py:127
  199.3 9.1 %all-to-all-start = ((bf16[8,32,1408]{2,1,0:T(8,128)(2,1)}), bf16[8,32,1408]{2,1,0:T(8,128)(2,1)S(1)}, u32[]{:S(2)}, u32[]{:S(2)}) async-start(bf16[8,32,1408]{2,1,0:T(8,128)(2,1)} %shard_map.30), calls=%async_computation | async-start | bytes 1441792 | tf_op jit(solution)/shard_map/all_to_all | solution.py:217
  208.4 3.7 %shard_map.37 = (f32[64,1408]{1,0:T(8,128)}, bf16[64,1408]{1,0:T(8,128)(2,1)}) custom-call(bf16[8,64,1408]{2,1,0:T(8,128)(2,1)} %copy-done), custom_call_target="tpu_custom_call" | custom-call | tf_op jit(solution)/shard_map/pallas_call | solution.py:154
  212.1 5.4 %collective-permute-start.4 = (bf16[64,1408]{1,0:T(8,128)(2,1)}, bf16[64,1408]{1,0:T(8,128)(2,1)S(1)}, u32[]{:S(2)}, u32[]{:S(2)}) collective-permute-start(bf16[64,1408]{1,0:T(8,128)(2,1)} %get-tuple-element.38), channel_id=1, source_target_pairs={{0,0},{2,16},{4,32},{6,48},{8,64},{10,80},{12,96},{14,112},{16,2},... | collective-permute-start | bytes 540680 | tf_op jit(solution)/shard_map/ppermute | solution.py:220
  217.6 3.7 %shard_map.35 = (f32[64,1408]{1,0:T(8,128)}, bf16[64,1408]{1,0:T(8,128)(2,1)}) custom-call(bf16[8,64,1408]{2,1,0:T(8,128)(2,1)} %copy-done.1), custom_call_target="tpu_custom_call" | custom-call | tf_op jit(solution)/shard_map/pallas_call | solution.py:154
  221.2 4.3 %collective-permute-start.3 = (bf16[64,1408]{1,0:T(8,128)(2,1)}, bf16[64,1408]{1,0:T(8,128)(2,1)S(1)}, u32[]{:S(2)}, u32[]{:S(2)}) collective-permute-start(bf16[64,1408]{1,0:T(8,128)(2,1)} %get-tuple-element.37), channel_id=1, source_target_pairs={{0,0},{2,16},{4,32},{6,48},{8,64},{10,80},{12,96},{14,112},{16,2},... | collective-permute-start | bytes 540680 | tf_op jit(solution)/shard_map/ppermute | solution.py:220
  225.5 3.7 %shard_map.33 = (f32[64,1408]{1,0:T(8,128)}, bf16[64,1408]{1,0:T(8,128)(2,1)}) custom-call(bf16[8,64,1408]{2,1,0:T(8,128)(2,1)} %copy-done.2), custom_call_target="tpu_custom_call" | custom-call | tf_op jit(solution)/shard_map/pallas_call | solution.py:154
  229.2 5.4 %collective-permute-start.2 = (bf16[64,1408]{1,0:T(8,128)(2,1)}, bf16[64,1408]{1,0:T(8,128)(2,1)S(1)}, u32[]{:S(2)}, u32[]{:S(2)}) collective-permute-start(bf16[64,1408]{1,0:T(8,128)(2,1)} %get-tuple-element.36), channel_id=1, source_target_pairs={{0,0},{2,16},{4,32},{6,48},{8,64},{10,80},{12,96},{14,112},{16,2},... | collective-permute-start | bytes 540680 | tf_op jit(solution)/shard_map/ppermute | solution.py:220
  234.7 10.8 %all-to-all-done.x_ref = bf16[8,32,1408]{2,1,0:T(8,128)(2,1)S(1)} async-done(((bf16[8,32,1408]{2,1,0:T(8,128)(2,1)}), bf16[8,32,1408]{2,1,0:T(8,128)(2,1)S(1)}, u32[]{:S(2)}, u32[]{:S(2)}) %all-to-all-start) | async-done | bytes 720928 | tf_op jit(solution)/shard_map/all_to_all | solution.py:217
  249.0 3.4 %collective-permute-start.1 = (bf16[32,1408]{1,0:T(8,128)(2,1)}, bf16[32,1408]{1,0:T(8,128)(2,1)S(1)}, u32[]{:S(2)}, u32[]{:S(2)}) collective-permute-start(bf16[32,1408]{1,0:T(8,128)(2,1)} %get-tuple-element.35), channel_id=1, source_target_pairs={{0,0},{2,16},{4,32},{6,48},{8,64},{10,80},{12,96},{14,112},{16,2},... | collective-permute-start | bytes 270344 | tf_op jit(solution)/shard_map/ppermute | solution.py:220
  252.4 7.1 %collective-permute-done.1.refs_4_ = bf16[32,1408]{1,0:T(8,128)(2,1)S(1)} collective-permute-done((bf16[32,1408]{1,0:T(8,128)(2,1)}, bf16[32,1408]{1,0:T(8,128)(2,1)S(1)}, u32[]{:S(2)}, u32[]{:S(2)}) %collective-permute-start.1) | collective-permute-done | bytes 90144 | tf_op jit(solution)/shard_map/ppermute | solution.py:220
  260.4 5.3 %shard_map.38 = f32[7,7,32,200]{3,2,1,0:T(8,128)} custom-call(f32[32,1408]{1,0:T(8,128)} %get-tuple-element.25.refs_0_, f32[64,1408]{1,0:T(8,128)} %get-tuple-element.28.refs_1_, f32[64,1408]{1,0:T(8,128)} %get-tuple-element.31.refs_2_, f32[64,1408]{1,0:T(8,128)} %get-tuple-element.34.refs_3_, bf16[32,1408]{1,0:T(8,128)(2,1)} %copy-done.7, ...), custom_call_target="tpu_custom_call" | custom-call | tf_op jit(solution)/shard_map/pallas_call | solution.py:185
  (33 shorter events, 8.5 us)
Async XLA Ops:
  6.5 39.4 %all-gather.15.cloned.1.call-start = ((), (), s32[]{:S(2)}) async-start(), calls=%async_computation.7 | async-start | bytes 3063808 | tf_op jit(solution)/shard_map/all_gather | solution.py:209
  8.6 87.4 %all-gather.13.cloned.1.call-start = ((), (), s32[]{:S(2)}) async-start(), calls=%async_computation.6 | async-start | bytes 3063808 | tf_op jit(solution)/shard_map/all_gather | solution.py:209
  9.4 137.1 %all-gather.11.cloned.1.call-start = ((), (), s32[]{:S(2)}) async-start(), calls=%async_computation.5 | async-start | bytes 3063808 | tf_op jit(solution)/shard_map/all_gather | solution.py:209
  26.3 7.3 %collective-permute-start = (bf16[1408,1408]{1,0:T(8,128)(2,1)}, bf16[1408,1408]{1,0:T(8,128)(2,1)}, u32[]{:S(2)}, u32[]{:S(2)}) collective-permute-start(bf16[1408,1408]{1,0:T(8,128)(2,1)} %get-tuple-element.24), channel_id=1, source_target_pairs={{0,1},{1,0},{2,3},{3,2},{4,5},{5,4},{6,7},{7,6},{8,9},{9,8},{10,11... | collective-permute-start | bytes 11894792 | tf_op jit(solution)/shard_map/ppermute | solution.py:211
  56.7 50.1 %all-to-all-start.3 = ((bf16[8,64,1408]{2,1,0:T(8,128)(2,1)}), bf16[8,64,1408]{2,1,0:T(8,128)(2,1)S(1)}, u32[]{:S(2)}, u32[]{:S(2)}) async-start(bf16[8,64,1408]{2,1,0:T(8,128)(2,1)} %shard_map.36), calls=%async_computation.3 | async-start | bytes 2883584 | tf_op jit(solution)/shard_map/all_to_all | solution.py:217
  63.9 127.5 %all-gather.9.cloned.1.call-start = ((), (), s32[]{:S(2)}) async-start(), calls=%async_computation.4 | async-start | bytes 1531904 | tf_op jit(solution)/shard_map/all_gather | solution.py:209
  106.8 50.5 %copy-start = (bf16[8,64,1408]{2,1,0:T(8,128)(2,1)}, bf16[8,64,1408]{2,1,0:T(8,128)(2,1)S(1)}, u32[]{:S(2)}) copy-start(bf16[8,64,1408]{2,1,0:T(8,128)(2,1)S(1)} %all-to-all-done.3.x_ref) | copy-start | bytes 4325380
  106.8 50.5 %all-to-all-start.2 = ((bf16[8,64,1408]{2,1,0:T(8,128)(2,1)}), bf16[8,64,1408]{2,1,0:T(8,128)(2,1)S(1)}, u32[]{:S(2)}, u32[]{:S(2)}) async-start(bf16[8,64,1408]{2,1,0:T(8,128)(2,1)} %shard_map.34), calls=%async_computation.2 | async-start | bytes 2883584 | tf_op jit(solution)/shard_map/all_to_all | solution.py:217
  157.3 41.9 %copy-start.1 = (bf16[8,64,1408]{2,1,0:T(8,128)(2,1)}, bf16[8,64,1408]{2,1,0:T(8,128)(2,1)S(1)}, u32[]{:S(2)}) copy-start(bf16[8,64,1408]{2,1,0:T(8,128)(2,1)S(1)} %all-to-all-done.2.x_ref) | copy-start | bytes 4325380
  157.3 41.9 %all-to-all-start.1 = ((bf16[8,64,1408]{2,1,0:T(8,128)(2,1)}), bf16[8,64,1408]{2,1,0:T(8,128)(2,1)S(1)}, u32[]{:S(2)}, u32[]{:S(2)}) async-start(bf16[8,64,1408]{2,1,0:T(8,128)(2,1)} %shard_map.32), calls=%async_computation.1 | async-start | bytes 2883584 | tf_op jit(solution)/shard_map/all_to_all | solution.py:217
  199.3 22.0 %copy-start.2 = (bf16[8,64,1408]{2,1,0:T(8,128)(2,1)}, bf16[8,64,1408]{2,1,0:T(8,128)(2,1)S(1)}, u32[]{:S(2)}) copy-start(bf16[8,64,1408]{2,1,0:T(8,128)(2,1)S(1)} %all-to-all-done.1.x_ref) | copy-start | bytes 4325380
  199.3 46.2 %all-to-all-start = ((bf16[8,32,1408]{2,1,0:T(8,128)(2,1)}), bf16[8,32,1408]{2,1,0:T(8,128)(2,1)S(1)}, u32[]{:S(2)}, u32[]{:S(2)}) async-start(bf16[8,32,1408]{2,1,0:T(8,128)(2,1)} %shard_map.30), calls=%async_computation | async-start | bytes 1441792 | tf_op jit(solution)/shard_map/all_to_all | solution.py:217
  212.1 47.4 %collective-permute-start.4 = (bf16[64,1408]{1,0:T(8,128)(2,1)}, bf16[64,1408]{1,0:T(8,128)(2,1)S(1)}, u32[]{:S(2)}, u32[]{:S(2)}) collective-permute-start(bf16[64,1408]{1,0:T(8,128)(2,1)} %get-tuple-element.38), channel_id=1, source_target_pairs={{0,0},{2,16},{4,32},{6,48},{8,64},{10,80},{12,96},{14,112},{16,2},... | collective-permute-start | bytes 540680 | tf_op jit(solution)/shard_map/ppermute | solution.py:220
  221.2 38.3 %collective-permute-start.3 = (bf16[64,1408]{1,0:T(8,128)(2,1)}, bf16[64,1408]{1,0:T(8,128)(2,1)S(1)}, u32[]{:S(2)}, u32[]{:S(2)}) collective-permute-start(bf16[64,1408]{1,0:T(8,128)(2,1)} %get-tuple-element.37), channel_id=1, source_target_pairs={{0,0},{2,16},{4,32},{6,48},{8,64},{10,80},{12,96},{14,112},{16,2},... | collective-permute-start | bytes 540680 | tf_op jit(solution)/shard_map/ppermute | solution.py:220
  229.2 30.3 %collective-permute-start.2 = (bf16[64,1408]{1,0:T(8,128)(2,1)}, bf16[64,1408]{1,0:T(8,128)(2,1)S(1)}, u32[]{:S(2)}, u32[]{:S(2)}) collective-permute-start(bf16[64,1408]{1,0:T(8,128)(2,1)} %get-tuple-element.36), channel_id=1, source_target_pairs={{0,0},{2,16},{4,32},{6,48},{8,64},{10,80},{12,96},{14,112},{16,2},... | collective-permute-start | bytes 540680 | tf_op jit(solution)/shard_map/ppermute | solution.py:220
  245.5 0.9 copy-start.3
  249.0 10.5 %collective-permute-start.1 = (bf16[32,1408]{1,0:T(8,128)(2,1)}, bf16[32,1408]{1,0:T(8,128)(2,1)S(1)}, u32[]{:S(2)}, u32[]{:S(2)}) collective-permute-start(bf16[32,1408]{1,0:T(8,128)(2,1)} %get-tuple-element.35), channel_id=1, source_target_pairs={{0,0},{2,16},{4,32},{6,48},{8,64},{10,80},{12,96},{14,112},{16,2},... | collective-permute-start | bytes 270344 | tf_op jit(solution)/shard_map/ppermute | solution.py:220
  259.5 0.6 copy-start.7
  259.5 0.7 copy-start.4
  259.5 0.8 copy-start.5
  259.5 0.8 copy-start.6
Sparse Core Ops, SparseCore 0:
  9.1 36.7 all-gather.14
  47.6 48.3 all-gather.12
  97.7 48.7 all-gather.10
  148.1 43.3 all-gather.8

commit v2 on v1

--- a/solution.py
+++ b/solution.py
@@ -5,10 +5,10 @@
 from jax.experimental.pallas import tpu as pltpu
 from jax.sharding import PartitionSpec as P
 
-CHUNKS = (1, 2, 2, 2)
+CHUNKS = (4, 3)
+RING = 4
 LANE = 128
 GAIN = 2.0**7.875
-VMEM = 60 * 1024 * 1024
 
 
 def padded(size):
@@ -19,8 +19,16 @@
     return pl.BlockSpec(memory_space=pltpu.VMEM)
 
 
-def params():
-    return pltpu.CompilerParams(vmem_limit_bytes=VMEM)
+def params(mib):
+    return pltpu.CompilerParams(vmem_limit_bytes=mib * 1024 * 1024)
+
+
+def cost(flops=0, moved=0):
+    return pl.CostEstimate(flops=flops, bytes_accessed=moved, transcendentals=0)
+
+
+def after(value, *arrays):
+    return lax.optimization_barrier((value, *arrays))[0]
 
 
 def encode(values, used):
@@ -64,7 +72,8 @@
         out_shape=[jax.ShapeDtypeStruct((count * width, lanes), x.dtype) for count in CHUNKS],
         in_specs=[whole()],
         out_specs=[whole() for _ in CHUNKS],
-        compiler_params=params(),
+        compiler_params=params(60),
+        cost_estimate=cost(moved=4 * x.size),
     )(x)
 
 
@@ -105,49 +114,100 @@
             in_specs=[pl.BlockSpec((1, outer, virt, wide), lambda k, s: (k, 0, 0, 0))],
             out_specs=[spec, spec],
         ),
-        compiler_params=params(),
+        compiler_params=params(60),
+        cost_estimate=cost(moved=8 * w.size),
     )(slab, w)
 
 
-def multiply(slab, gathered, mine, other, used):
-    blocks, slabs, rows, _ = gathered.shape
+def multiply(places, gathered, rings, mine, other, used, apart):
     depth, lanes = mine.shape
-    per_step = max(1, 256 // rows)
-
-    def kernel(slab_ref, g_ref, mine_ref, other_ref, out_ref):
-        own = slab_ref[0]
-
-        def part(which):
-            return g_ref[:, pl.ds(which, 1), :, :].reshape(per_step * rows, depth)
-
-        total = jnp.dot(part(own), mine_ref[...], preferred_element_type=jnp.float32)
-        total += jnp.dot(part(1 - own), other_ref[...], preferred_element_type=jnp.float32)
-        out_ref[...] = encode(total, used).reshape(per_step, rows, lanes)
-
-    return pl.pallas_call(
-        kernel,
-        out_shape=jax.ShapeDtypeStruct((blocks, rows, lanes), jnp.bfloat16),
-        grid_spec=pltpu.PrefetchScalarGridSpec(
-            num_scalar_prefetch=1,
-            grid=(blocks // per_step,),
-            in_specs=[
-                pl.BlockSpec((per_step, slabs, rows, gathered.shape[3]), lambda n, s: (n, 0, 0, 0)),
-                pl.BlockSpec((depth, lanes), lambda n, s: (0, 0)),
-                pl.BlockSpec((depth, lanes), lambda n, s: (0, 0)),
-            ],
-            out_specs=pl.BlockSpec((per_step, rows, lanes), lambda n, s: (n, 0, 0)),
-        ),
-        compiler_params=params(),
-    )(slab, gathered, mine, other)
-
-
-def add_up(received, used):
-    blocks, rows, lanes = received.shape
-
-    def kernel(x_ref, sum_ref, coded_ref):
-        total = decode(x_ref[0], used)
-        for n in range(1, blocks):
-            total += decode(x_ref[n], used)
+    rows = gathered.shape[-2]
+    count = gathered.shape[0] * (gathered.shape[2] if rings else 1)
+    group = RING if rings else max(1, min(count, 256 // rows))
+
+    def kernel(slab_ref, ring_ref, dest_ref, g_ref, mine_ref, other_ref, *refs):
+        out_refs, (total, left, right, mine_buf, other_buf, sems) = refs[:-6], refs[-6:]
+        moves = [[(mine_ref, mine_buf)], [(other_ref, other_buf)]]
+        for side, buf in enumerate((left, right)):
+            which = slab_ref[0] if side == 0 else 1 - slab_ref[0]
+            if rings:
+                for n in range(count // RING):
+                    moves[side].append((g_ref.at[:, which, n], buf.at[n * RING : (n + 1) * RING]))
+            else:
+                moves[side].append((g_ref.at[:, which], buf))
+        copies, n = [[], []], 0
+        for side in range(2):
+            for src, dst in moves[side]:
+                copies[side].append(pltpu.make_async_copy(src, dst, sems.at[n]))
+                copies[side][-1].start()
+                n += 1
+
+        def product(start, rows_ref, buf):
+            block = rows_ref[start : start + group].reshape(group * rows, depth)
+            return jnp.dot(block, buf[...], preferred_element_type=jnp.float32).reshape(group, rows, lanes)
+
+        def place(start):
+            if not rings:
+                return slice(start, start + group)
+            ring = ring_ref[0] if start == 0 else 1 - ring_ref[0]
+            return pl.ds(ring * RING, RING)
+
+        for copy in copies[0]:
+            copy.wait()
+        for start in range(0, count, group):
+            total[place(start)] = product(start, left, mine_buf)
+        for copy in copies[1]:
+            copy.wait()
+        for start in range(0, count, group):
+            block = total[place(start)] + product(start, right, other_buf)
+            if apart:
+                total[place(start)] = block
+            else:
+                coded = encode(block.reshape(group * rows, lanes), used)
+                out_refs[0][place(start)] = coded.reshape(group, rows, lanes)
+        if apart:
+            out_refs[0][...] = total[dest_ref[0]]
+            for n, out_ref in enumerate(out_refs[1:]):
+                out_ref[...] = encode(total[dest_ref[n + 1]], used)
+
+    if apart:
+        shapes = [jax.ShapeDtypeStruct((rows, lanes), jnp.float32)]
+        shapes += [jax.ShapeDtypeStruct((rows, lanes), jnp.bfloat16)] * (count - 1)
+    else:
+        shapes = [jax.ShapeDtypeStruct((count, rows, lanes), jnp.bfloat16)]
+    smem, hbm = pl.BlockSpec(memory_space=pltpu.SMEM), pl.BlockSpec(memory_space=pl.ANY)
+    return pl.pallas_call(
+        kernel,
+        out_shape=shapes,
+        in_specs=[smem] * 3 + [hbm] * 3,
+        out_specs=[whole() for _ in shapes],
+        scratch_shapes=[
+            pltpu.VMEM((count, rows, lanes), jnp.float32),
+            pltpu.VMEM((count, rows, depth), mine.dtype),
+            pltpu.VMEM((count, rows, depth), mine.dtype),
+            pltpu.VMEM(mine.shape, mine.dtype),
+            pltpu.VMEM(other.shape, other.dtype),
+            pltpu.SemaphoreType.DMA((2 + (count // RING) * 2,)),
+        ],
+        compiler_params=params(60),
+        cost_estimate=cost(flops=4 * count * rows * depth * lanes, moved=8 * depth * lanes),
+    )(*places, gathered, mine, other)
+
+
+def add_up(parts, used):
+    rows, lanes = parts[0].shape[-2:]
+
+    def kernel(*refs):
+        sum_ref, coded_ref = refs[-2:]
+        total = 0.0
+        for ref in refs[:-2]:
+            if len(ref.shape) == 3:
+                for n in range(ref.shape[0]):
+                    total += decode(ref[n], used)
+            elif ref.dtype == jnp.float32:
+                total += ref[...]
+            else:
+                total += decode(ref[...], used)
         sum_ref[...] = total
         coded_ref[...] = encode(total, used)
 
@@ -157,10 +217,11 @@
             jax.ShapeDtypeStruct((rows, lanes), jnp.float32),
             jax.ShapeDtypeStruct((rows, lanes), jnp.bfloat16),
         ],
-        in_specs=[whole()],
+        in_specs=[whole() for _ in parts],
         out_specs=[whole(), whole()],
-        compiler_params=params(),
-    )(received)
+        compiler_params=params(60),
+        cost_estimate=cost(moved=64 * rows * lanes),
+    )(*parts)
 
 
 def subtract(sums, mirrored, width, occ, virt):
@@ -188,8 +249,20 @@
         in_specs=[whole() for _ in range(2 * count)],
         out_specs=whole(),
         scratch_shapes=[pltpu.VMEM((occ * width, sums[0].shape[1]), jnp.float32)],
-        compiler_params=params(),
+        compiler_params=params(60),
+        cost_estimate=cost(moved=32 * occ * occ * width * virt),
     )(*sums, *mirrored)
+
+
+def distances(size):
+    halves = size // RING
+    return [(0, 0)] + [(h, s) for h in range(halves - 1, -1, -1) for s in (2, 1, -1, 0) if (h, s) != (0, 0)]
+
+
+def moved(place, size, distance):
+    half, step = distance
+    ring = place // RING
+    return (ring + half) % (size // RING) * RING + (place % RING + step) % RING
 
 
 def on_device(amplitudes, integrals):
@@ -200,22 +273,35 @@
     rows, cols = lax.axis_size("row"), lax.axis_size("col")
     slab = lax.axis_index("slab").astype(jnp.int32).reshape(1)
     mirror_pairs = [(r * cols + c, c * cols + r) for r in range(rows) for c in range(cols)]
-
-    packed = pack_amplitudes(jnp.transpose(amplitudes, (0, 2, 1, 3)))
-    gathered = []
-    for chunk in packed:
-        if gathered:
-            chunk, _ = lax.optimization_barrier((chunk, gathered[-1]))
-        gathered.append(lax.all_gather(chunk, ("col", "slab"), axis=0))
-    mine, sent = pack_integrals(slab, jnp.transpose(integrals, (0, 2, 1, 3)))
-    other = lax.ppermute(sent, "slab", [(0, 1), (1, 0)])
+    apart = distances(rows)
+    row = lax.axis_index("row").astype(jnp.int32)
+    dest = jnp.stack([moved(row, rows, distance) for distance in apart])
+
+    ring = (lax.axis_index("col") // RING).astype(jnp.int32).reshape(1)
+    places = (slab, ring, dest)
+    swap = [(0, 1), (1, 0)]
+    cross = [(c, (c + RING) % cols) for c in range(cols)]
+    groups = [list(range(n, n + 2 * RING)) for n in range(0, 2 * cols, 2 * RING)]
+
+    packed, rest = pack_amplitudes(jnp.transpose(amplitudes, (0, 2, 1, 3)))
+    early = lax.all_gather(packed, ("col", "slab"), axis=0)
+    early = early.reshape(cols, 2, *packed.shape)
+    mine, sent = pack_integrals(after(slab, packed), jnp.transpose(integrals, (0, 2, 1, 3)))
+    other = lax.ppermute(sent, "slab", swap)
+    pair = jnp.stack([rest, lax.ppermute(after(rest, other), "col", cross)])
+    late = lax.all_gather(after(pair, early), ("col", "slab"), axis=0, axis_index_groups=groups)
+    late = late.reshape(RING, 2, *pair.shape)
+
+    shares = []
+    for source, rings in ((early, False), (late, True)):
+        (coded,) = multiply(places, source, rings, mine, other, used, False)
+        shares.append([lax.all_to_all(coded, "row", 0, 0, tiled=True)])
 
     sums, mirrored = [], []
-    for chunk in gathered:
-        chunk = chunk.reshape(cols, 2, chunk.shape[1], chunk.shape[2])
-        coded = multiply(slab, chunk, mine, other, used)
-        received = lax.all_to_all(coded, "row", 0, 0, tiled=True)
-        total, again = add_up(received, used)
+    for parts in shares:
+        if sums:
+            parts = list(lax.optimization_barrier((*parts, sums[-1]))[:-1])
+        total, again = add_up(parts, used)
         sums.append(total)
         mirrored.append(lax.ppermute(again, ("row", "col"), mirror_pairs))
     residual = subtract(sums, mirrored, width, occ, out_virt)

time: 273 us -> 204 us (0.75)
  waiting for transfers between devices: 130 us -> 95.9 us
  starting transfers between devices: 50.2 us -> 27.1 us
  Pallas kernels: 77.5 us -> 65.1 us
    all_gather x4 -> x2, waiting for transfers between devices: 102 us -> 17.5 us  [the longest x1 9.08 us: on_device(): early = lax.all_gather(packed, ('col', 'slab'), axis=0)]
    all_to_all x4 -> x2, waiting for transfers between devices: 10.8 us -> 49.6 us  [on_device(): shares.append([lax.all_to_all(coded, 'row', 0, 0, tiled=True)])]
    all_to_all x4 -> x2, starting transfers between devices: 31.6 us -> 15.9 us  [on_device(): shares.append([lax.all_to_all(coded, 'row', 0, 0, tiled=True)])]
    ppermute x1 -> x2, waiting for transfers between devices: 7.3 us -> 20.2 us  [the longest x1 12.8 us: on_device(): pair = jnp.stack([rest, lax.ppermute(after(rest, other), 'col', cross)])]
    pallas_call x4 -> x2, Pallas kernels: 40.3 us -> 30.9 us  [multiply(): pl.pallas_call(kernel, out_shape=shapes, in_specs=[smem] * 3 + [hbm] * 3,...]
    ppermute x4 -> x2, starting transfers between devices: 18.6 us -> 9.31 us  [on_device(): mirrored.append(lax.ppermute(again, ('row', 'col'), mirror_pairs))]
    pallas_call x4 -> x2, Pallas kernels: 13.7 us -> 10.6 us  [add_up(): pl.pallas_call(kernel, out_shape=[jax.ShapeDtypeStruct((rows, lanes), jnp...]
    ppermute x4 -> x2, waiting for transfers between devices: 7.14 us -> 8.57 us  [on_device(): mirrored.append(lax.ppermute(again, ('row', 'col'), mirror_pairs))]
  transfers between devices with their start and end apart: 13 -> 8, of which waited for: 7 -> 7; matrix products, arithmetic and copies ran while one was open for 0% -> 1% of each run, Pallas kernels for 26% -> 28%
where the time goes in v2:
time: 204 us
  waiting for transfers between devices  95.9 us (47%)
  Pallas kernels  65.1 us (32%)
  starting transfers between devices  27.1 us (13%)
  between operations  13.6 us (7%)
    all_to_all x2, waiting for transfers between devices, on_device(): shares.append([lax.all_to_all(coded, 'row', 0, 0, tiled=True)])  49.6 us
    pallas_call x2, Pallas kernels, multiply(): pl.pallas_call(kernel, out_shape=shapes, in_specs=[smem] * 3 + [hbm] * 3,...  30.9 us
    pallas_call x1, Pallas kernels, pack_integrals(): pl.pallas_call(kernel, out_shape=[shape, shape], grid_spec=pltpu.Prefetch...  16.2 us
    all_to_all x2, starting transfers between devices, on_device(): shares.append([lax.all_to_all(coded, 'row', 0, 0, tiled=True)])  15.9 us
    ppermute x1, waiting for transfers between devices, on_device(): pair = jnp.stack([rest, lax.ppermute(after(rest, other), 'col', cross)])  12.8 us
    pallas_call x2, Pallas kernels, add_up(): pl.pallas_call(kernel, out_shape=[jax.ShapeDtypeStruct((rows, lanes), jnp...  10.6 us
    ppermute x2, starting transfers between devices, on_device(): mirrored.append(lax.ppermute(again, ('row', 'col'), mirror_pairs))  9.31 us
    all_gather x1, waiting for transfers between devices, on_device(): early = lax.all_gather(packed, ('col', 'slab'), axis=0)  9.08 us
  transfers between devices with their start and end apart: 8, of which 7 were waited for; matrix products, arithmetic and copies ran while one was open for 1% of the time, Pallas kernels for 28%

profile of v2, /device:TPU:14, one launch (start us, length us, event | category | flops | bytes accessed | tf_op | source)
XLA Modules:
  0.0 203.9 jit_solution(6595529291506302941)
XLA Ops:
  6.5 2.1 %shard_map.28 = (bf16[128,1408]{1,0:T(8,128)(2,1)}, bf16[96,1408]{1,0:T(8,128)(2,1)}) custom-call(bf16[7,7,32,200]{3,2,1,0:T(8,128)(2,1)} %bitcast.18), custom_call_target="tpu_custom_call" | custom-call | bytes 1254400 | tf_op jit(solution)/shard_map/pallas_call | solution.py:70
  8.7 0.0 all-gather.5.cloned.1.call-update
  8.7 0.0 all-gather.7.cloned.1.call-start
  8.8 16.2 %shard_map.29 = (bf16[1408,1408]{1,0:T(8,128)(2,1)}, bf16[1408,1408]{1,0:T(8,128)(2,1)}) custom-call(s32[1]{0:T(128)} %bitcast.slab_ref, bf16[7,7,200,400]{3,2,1,0:T(8,128)(2,1)} %bitcast.17), custom_call_target="tpu_custom_call" | custom-call | bytes 31360000 | tf_op jit(solution)/shard_map/pallas_call | solution.py:108
  24.9 7.4 %collective-permute-done.other_ref = bf16[1408,1408]{1,0:T(8,128)(2,1)S(1)} collective-permute-done((bf16[1408,1408]{1,0:T(8,128)(2,1)}, bf16[1408,1408]{1,0:T(8,128)(2,1)S(1)}, u32[]{:S(2)}, u32[]{:S(2)}) %collective-permute-start) | collective-permute-done | bytes 3964960 | tf_op jit(solution)/shard_map/ppermute | solution.py:290
  32.3 1.8 collective-permute-start.1
  34.1 12.8 %collective-permute-done.1 = bf16[96,1408]{1,0:T(8,128)(2,1)S(1)} collective-permute-done((bf16[96,1408]{1,0:T(8,128)(2,1)S(1)}, bf16[96,1408]{1,0:T(8,128)(2,1)S(1)}, u32[]{:S(2)}, u32[]{:S(2)}) %collective-permute-start.1) | collective-permute-done | bytes 270368 | tf_op jit(solution)/shard_map/ppermute | solution.py:291
  46.9 0.9 pad_maximum_fusion
  47.8 9.1 %all-gather.5.cloned.1.call-done = bf16[2048,1408]{1,0:T(8,128)(2,1)} async-done(((bf16[128,1408]{1,0:T(8,128)(2,1)}), bf16[2048,1408]{1,0:T(8,128)(2,1)}) %all-gather.5.cloned.1.call-update) | async-done | bytes 5767184 | tf_op jit(solution)/shard_map/all_gather | solution.py:287
  57.0 0.6 stack.44.dest_ref
  57.7 17.0 %shard_map.30 = bf16[8,128,1408]{2,1,0:T(8,128)(2,1)} custom-call(s32[1]{0:T(128)} %bitcast.slab_ref, s32[1]{0:T(128)} %bitcast.1.ring_ref, s32[8]{0:T(128)} %stack.44.dest_ref, bf16[8,2,128,1408]{3,2,1,0:T(8,128)(2,1)} %bitcast.21, bf16[1408,1408]{1,0:T(8,128)(2,1)} %get-tuple-element.19.mine_ref, bf16[1408,1408]{1,0:T(8,128)(2,1)} %copy-done.4), custom_call_target="tpu_custom_call" | custom-call | flops 8120172544 | bytes 15859712 | tf_op jit(solution)/shard_map/pallas_call | solution.py:179
  74.7 7.1 %all-to-all-start = ((bf16[8,128,1408]{2,1,0:T(8,128)(2,1)}), bf16[8,128,1408]{2,1,0:T(8,128)(2,1)S(1)}, u32[]{:S(2)}, u32[]{:S(2)}) async-start(bf16[8,128,1408]{2,1,0:T(8,128)(2,1)} %shard_map.30), calls=%async_computation | async-start | bytes 5767168 | tf_op jit(solution)/shard_map/all_to_all | solution.py:298
  81.8 8.5 %all-gather.7.cloned.1.call-done = bf16[16,96,1408]{2,1,0:T(8,128)(2,1)} async-done(((bf16[2,96,1408]{2,1,0:T(8,128)(2,1)}), bf16[16,96,1408]{2,1,0:T(8,128)(2,1)}) %all-gather.7.cloned.1.call-update) | async-done | bytes 4325392 | tf_op jit(solution)/shard_map/all_gather | solution.py:292
  90.3 13.9 %shard_map.32 = bf16[8,96,1408]{2,1,0:T(8,128)(2,1)} custom-call(s32[1]{0:T(128)} %bitcast.slab_ref, s32[1]{0:T(128)} %bitcast.1.ring_ref, s32[8]{0:T(128)} %stack.44.dest_ref, bf16[4,2,2,96,1408]{4,3,2,1,0:T(8,128)(2,1)} %bitcast.22, bf16[1408,1408]{1,0:T(8,128)(2,1)} %get-tuple-element.19.mine_ref, bf16[1408,1408]{1,0:T(8,128)(2,1)} %copy-done.4), custom_call_target="tpu_custom_call" | custom-call | flops 6090129408 | bytes 15859712 | tf_op jit(solution)/shard_map/pallas_call | solution.py:179
  104.2 18.1 %all-to-all-done.refs_0_ = bf16[8,128,1408]{2,1,0:T(8,128)(2,1)S(1)} async-done(((bf16[8,128,1408]{2,1,0:T(8,128)(2,1)}), bf16[8,128,1408]{2,1,0:T(8,128)(2,1)S(1)}, u32[]{:S(2)}, u32[]{:S(2)}) %all-to-all-start) | async-done | bytes 2883616 | tf_op jit(solution)/shard_map/all_to_all | solution.py:298
  122.3 8.8 %all-to-all-start.1 = ((bf16[8,96,1408]{2,1,0:T(8,128)(2,1)}), bf16[8,96,1408]{2,1,0:T(8,128)(2,1)}, u32[]{:S(2)}, u32[]{:S(2)}) async-start(bf16[8,96,1408]{2,1,0:T(8,128)(2,1)} %shard_map.32), calls=%async_computation.1 | async-start | bytes 4325376 | tf_op jit(solution)/shard_map/all_to_all | solution.py:298
  131.1 5.8 %shard_map.31 = (f32[128,1408]{1,0:T(8,128)}, bf16[128,1408]{1,0:T(8,128)(2,1)}) custom-call(bf16[8,128,1408]{2,1,0:T(8,128)(2,1)} %copy-done), custom_call_target="tpu_custom_call" | custom-call | bytes 11534336 | tf_op jit(solution)/shard_map/pallas_call | solution.py:214
  136.9 5.4 %collective-permute-start.2 = (bf16[128,1408]{1,0:T(8,128)(2,1)}, bf16[128,1408]{1,0:T(8,128)(2,1)S(1)}, u32[]{:S(2)}, u32[]{:S(2)}) collective-permute-start(bf16[128,1408]{1,0:T(8,128)(2,1)} %get-tuple-element.27), channel_id=1, source_target_pairs={{0,0},{2,16},{4,32},{6,48},{8,64},{10,80},{12,96},{14,112},{16,2},... | collective-permute-start | bytes 1081352 | tf_op jit(solution)/shard_map/ppermute | solution.py:306
  142.3 31.5 %all-to-all-done.1.refs_0_ = bf16[8,96,1408]{2,1,0:T(8,128)(2,1)} async-done(((bf16[8,96,1408]{2,1,0:T(8,128)(2,1)}), bf16[8,96,1408]{2,1,0:T(8,128)(2,1)}, u32[]{:S(2)}, u32[]{:S(2)}) %all-to-all-start.1) | async-done | bytes 2162720 | tf_op jit(solution)/shard_map/all_to_all | solution.py:298
  173.8 4.8 %shard_map.33 = (f32[96,1408]{1,0:T(8,128)}, bf16[96,1408]{1,0:T(8,128)(2,1)}) custom-call(bf16[8,96,1408]{2,1,0:T(8,128)(2,1)} %all-to-all-done.1.refs_0_), custom_call_target="tpu_custom_call" | custom-call | bytes 8650752 | tf_op jit(solution)/shard_map/pallas_call | solution.py:214
  178.6 3.9 %collective-permute-start.3 = (bf16[96,1408]{1,0:T(8,128)(2,1)}, bf16[96,1408]{1,0:T(8,128)(2,1)S(1)}, u32[]{:S(2)}, u32[]{:S(2)}) collective-permute-start(bf16[96,1408]{1,0:T(8,128)(2,1)} %get-tuple-element.28), channel_id=1, source_target_pairs={{0,0},{2,16},{4,32},{6,48},{8,64},{10,80},{12,96},{14,112},{16,2},... | collective-permute-start | bytes 811016 | tf_op jit(solution)/shard_map/ppermute | solution.py:306
  182.5 8.6 %collective-permute-done.3.refs_3_ = bf16[96,1408]{1,0:T(8,128)(2,1)S(1)} collective-permute-done((bf16[96,1408]{1,0:T(8,128)(2,1)}, bf16[96,1408]{1,0:T(8,128)(2,1)S(1)}, u32[]{:S(2)}, u32[]{:S(2)}) %collective-permute-start.3) | collective-permute-done | bytes 270368 | tf_op jit(solution)/shard_map/ppermute | solution.py:306
  191.1 0.7 copy-done.3
  191.8 5.3 %shard_map.34 = f32[7,7,32,200]{3,2,1,0:T(8,128)} custom-call(f32[128,1408]{1,0:T(8,128)} %get-tuple-element.21.refs_0_, f32[96,1408]{1,0:T(8,128)} %get-tuple-element.26.refs_1_, bf16[128,1408]{1,0:T(8,128)(2,1)} %copy-done.1, bf16[96,1408]{1,0:T(8,128)(2,1)} %copy-done.3), custom_call_target="tpu_custom_call" | custom-call | bytes 10035200 | tf_op jit(solution)/shard_map/pallas_call | solution.py:246
  (13 shorter events, 0.0 us)
Async XLA Ops:
  6.5 50.3 %all-gather.5.cloned.1.call-start = ((), (), s32[]{:S(2)}) async-start(), calls=%async_computation.2 | async-start | bytes 6127616 | tf_op jit(solution)/shard_map/all_gather | solution.py:287
  8.7 81.6 %all-gather.7.cloned.1.call-start = ((), (), s32[]{:S(2)}) async-start(), calls=%async_computation.3 | async-start | bytes 4866048 | tf_op jit(solution)/shard_map/all_gather | solution.py:292
  8.7 23.6 %copy-start.2 = (bf16[96,1408]{1,0:T(8,128)(2,1)S(1)}, bf16[96,1408]{1,0:T(8,128)(2,1)}, u32[]{:S(2)}) copy-start(bf16[96,1408]{1,0:T(8,128)(2,1)} %get-tuple-element.23) | copy-start | bytes 811012
  24.9 7.4 %collective-permute-start = (bf16[1408,1408]{1,0:T(8,128)(2,1)}, bf16[1408,1408]{1,0:T(8,128)(2,1)S(1)}, u32[]{:S(2)}, u32[]{:S(2)}) collective-permute-start(bf16[1408,1408]{1,0:T(8,128)(2,1)} %get-tuple-element.20), channel_id=1, source_target_pairs={{0,1},{1,0},{2,3},{3,2},{4,5},{5,4},{6,7},{7,6},{8,9},{9,8},{10,11... | collective-permute-start | bytes 11894792 | tf_op jit(solution)/shard_map/ppermute | solution.py:290
  32.3 14.6 %copy-start.4 = (bf16[1408,1408]{1,0:T(8,128)(2,1)}, bf16[1408,1408]{1,0:T(8,128)(2,1)S(1)}, u32[]{:S(2)}) copy-start(bf16[1408,1408]{1,0:T(8,128)(2,1)S(1)} %collective-permute-done.other_ref) | copy-start | bytes 11894788
  32.3 14.6 %collective-permute-start.1 = (bf16[96,1408]{1,0:T(8,128)(2,1)S(1)}, bf16[96,1408]{1,0:T(8,128)(2,1)S(1)}, u32[]{:S(2)}, u32[]{:S(2)}) collective-permute-start(bf16[96,1408]{1,0:T(8,128)(2,1)S(1)} %copy-done.2), channel_id=1, source_target_pairs={{0,8},{2,10},{4,12},{6,14},{8,0},{10,2},{12,4},{14,6},{1,9},{3,11}... | collective-permute-start | bytes 811016 | tf_op jit(solution)/shard_map/ppermute | solution.py:291
  74.7 47.6 %all-to-all-start = ((bf16[8,128,1408]{2,1,0:T(8,128)(2,1)}), bf16[8,128,1408]{2,1,0:T(8,128)(2,1)S(1)}, u32[]{:S(2)}, u32[]{:S(2)}) async-start(bf16[8,128,1408]{2,1,0:T(8,128)(2,1)} %shard_map.30), calls=%async_computation | async-start | bytes 5767168 | tf_op jit(solution)/shard_map/all_to_all | solution.py:298
  122.3 8.8 %copy-start = (bf16[8,128,1408]{2,1,0:T(8,128)(2,1)}, bf16[8,128,1408]{2,1,0:T(8,128)(2,1)S(1)}, u32[]{:S(2)}) copy-start(bf16[8,128,1408]{2,1,0:T(8,128)(2,1)S(1)} %all-to-all-done.refs_0_) | copy-start | bytes 8650756
  122.3 51.5 %all-to-all-start.1 = ((bf16[8,96,1408]{2,1,0:T(8,128)(2,1)}), bf16[8,96,1408]{2,1,0:T(8,128)(2,1)}, u32[]{:S(2)}, u32[]{:S(2)}) async-start(bf16[8,96,1408]{2,1,0:T(8,128)(2,1)} %shard_map.32), calls=%async_computation.1 | async-start | bytes 4325376 | tf_op jit(solution)/shard_map/all_to_all | solution.py:298
  136.9 45.6 %collective-permute-start.2 = (bf16[128,1408]{1,0:T(8,128)(2,1)}, bf16[128,1408]{1,0:T(8,128)(2,1)S(1)}, u32[]{:S(2)}, u32[]{:S(2)}) collective-permute-start(bf16[128,1408]{1,0:T(8,128)(2,1)} %get-tuple-element.27), channel_id=1, source_target_pairs={{0,0},{2,16},{4,32},{6,48},{8,64},{10,80},{12,96},{14,112},{16,2},... | collective-permute-start | bytes 1081352 | tf_op jit(solution)/shard_map/ppermute | solution.py:306
  178.6 12.5 %collective-permute-start.3 = (bf16[96,1408]{1,0:T(8,128)(2,1)}, bf16[96,1408]{1,0:T(8,128)(2,1)S(1)}, u32[]{:S(2)}, u32[]{:S(2)}) collective-permute-start(bf16[96,1408]{1,0:T(8,128)(2,1)} %get-tuple-element.28), channel_id=1, source_target_pairs={{0,0},{2,16},{4,32},{6,48},{8,64},{10,80},{12,96},{14,112},{16,2},... | collective-permute-start | bytes 811016 | tf_op jit(solution)/shard_map/ppermute | solution.py:306
  182.5 8.6 %copy-start.1 = (bf16[128,1408]{1,0:T(8,128)(2,1)}, bf16[128,1408]{1,0:T(8,128)(2,1)S(1)}, u32[]{:S(2)}) copy-start(bf16[128,1408]{1,0:T(8,128)(2,1)S(1)} %collective-permute-done.2.refs_2_) | copy-start | bytes 1081348
  191.0 0.7 copy-start.3
Sparse Core Ops, SparseCore 0:
  9.1 47.7 all-gather.4
  58.6 31.6 all-gather.6
